TPU v7x, 256 devices: a whole 4x4x8 slice. The times are simulated.
256 devices in a mesh: row: 8 (over x, y_hi), col: 8 (over z), depth: 4 (over y_lo, core).
Axes of the slice: x: 4, y: 4 (y_hi: 2, y_lo: 2; y = y_hi * 2 + y_lo), z: 8, core: 2. Of those that a mesh axis runs over, the one named last changes fastest.
Arguments:
- context: bfloat16 [16384, 4096], P(('row', 'depth'), 'col'), may hold values from -6 to 6
- out_grad: bfloat16 [16384, 5120], P(('row', 'depth'), 'col'), may hold values from -6 to 6
- master: float32 [4096, 5120], P('row', 'col'), may hold values from -0.09375 to 0.09375
- first_moment: float32 [4096, 5120], P('row', 'col'), may hold values from -384 to 384
- second_moment: float32 [4096, 5120], P('row', 'col'), may hold values from 1638.4 to 163840
Outputs:
- input_grad: bfloat16 [16384, 4096], P(('row', 'depth'), 'col')
- new_master: float32 [4096, 5120], P('row', 'col')
- new_first: float32 [4096, 5120], P('row', 'col')
- new_second: float32 [4096, 5120], P('row', 'col')
All inputs are finite; a program needn't handle non-finite values.
Results may differ from a plain program's by a relative error of at most 0.017.
Values may be sent and summed in bfloat16 or wider, within the bound.
A program may use at most 64 MiB of HBM per device.

v0:
```python
import jax
import jax.numpy as jnp
from jax import lax
from jax.sharding import PartitionSpec as P

STEP = 10


beta_one = 0.9
beta_two = 0.95
adam_eps = 1e-08
learn_rate = 0.001
decay_rate = 0.1


def adam_update(gradient, master, first_moment, second_moment):
    new_first = beta_one * first_moment + (1.0 - beta_one) * gradient
    new_second = beta_two * second_moment + (1.0 - beta_two) * gradient * gradient
    first_hat = new_first / (1.0 - beta_one**STEP)
    second_hat = new_second / (1.0 - beta_two**STEP)
    new_master = master - learn_rate * (
        first_hat / (jnp.sqrt(second_hat) + adam_eps) + decay_rate * master
    )
    return (new_master, new_first, new_second)


def on_device(context, out_grad, master, first_moment, second_moment):
    weight = master.astype(jnp.bfloat16)
    partial_terms = lax.dot_general(
        out_grad,
        lax.all_gather(weight, "row", axis=0, tiled=True),
        (((1,), (1,)), ((), ())),
        preferred_element_type=jnp.float32,
    )
    input_grad = lax.psum_scatter(
        partial_terms.astype(jnp.bfloat16), "col", scatter_dimension=1, tiled=True
    )
    gathered = lax.all_gather(context, "col", axis=1, tiled=True)
    grad_share = lax.psum_scatter(
        lax.dot_general(
            gathered, out_grad, (((0,), (0,)), ((), ())), preferred_element_type=jnp.float32
        ).astype(jnp.bfloat16),
        ("row", "depth"),
        scatter_dimension=0,
        tiled=True,
    ).astype(jnp.float32)
    gradient = lax.all_gather(grad_share.astype(jnp.bfloat16), "depth", axis=0, tiled=True).astype(
        grad_share.dtype
    )
    new_master, new_first, new_second = adam_update(gradient, master, first_moment, second_moment)
    return (input_grad, new_master, new_first, new_second)


def solution(mesh):
    in_specs = (
        P(("row", "depth"), "col"),
        P(("row", "depth"), "col"),
        P("row", "col"),
        P("row", "col"),
        P("row", "col"),
    )
    out_specs = (P(("row", "depth"), "col"), P("row", "col"), P("row", "col"), P("row", "col"))
    return jax.shard_map(
        on_device, mesh=mesh, in_specs=in_specs, out_specs=out_specs, check_vma=False
    )
```

profile of v0, /device:TPU:5, one launch (start us, length us, event | category | flops | bytes accessed | tf_op | source)
XLA Modules:
  0.0 331.1 jit_solution(10853040313704571219)
XLA Ops:
  7.2 0.0 copy-start
  7.2 0.0 all-gather.5.cloned.1.call-start
  7.2 0.7 all-gather.5.cloned.1.call-update
  7.9 0.0 reduce-scatter.5.cloned.1.call-start
  8.0 59.6 %all-gather.5.cloned.1.call-done = bf16[512,4096]{1,0:T(8,128)(2,1)} async-done(((bf16[512,512]{1,0:T(8,128)(2,1)}), bf16[512,4096]{1,0:T(8,128)(2,1)}) %all-gather.5.cloned.1.call-update) | async-done | bytes 4194320 | tf_op jit(solution)/shard_map/all_gather | solution.py:38
  67.6 0.0 copy-done
  67.6 8.0 %convolution_convert_fusion = bf16[4096,640]{1,0:T(8,128)(2,1)} fusion(bf16[512,4096]{1,0:T(8,128)(2,1)} %all-gather.5.cloned.1.call-done, bf16[512,640]{1,0:T(8,128)(2,1)S(1)} %copy-done), kind=kOutput, calls=%fused_computation | convolution fusion | flops 2686976000 | bytes 10092544 | tf_op jit(solution)/shard_map/dot_general | solution.py:40
  75.6 0.0 copy-start.1
  75.6 0.0 copy-start.2
  75.6 0.0 reduce-scatter.5.cloned.1.call-update
  75.6 0.0 all-gather.3.cloned.1.call-start
  75.6 88.4 %reduce-scatter.5.cloned.1.call-done = bf16[128,640]{1,0:T(8,128)(2,1)} async-done(((bf16[4096,640]{1,0:T(8,128)(2,1)}), bf16[128,640]{1,0:T(8,128)(2,1)}) %reduce-scatter.5.cloned.1.call-update) | async-done | bytes 163856 | tf_op jit(solution)/shard_map/reduce_scatter | solution.py:39
  164.0 9.9 %all_gather.11 = bf16[512,640]{1,0:T(8,128)(2,1)S(1)} all-gather(bf16[128,640]{1,0:T(8,128)(2,1)} %reduce-scatter.5.cloned.1.call-done), channel_id=1, replica_groups=mesh['row'=8,'col'=8,'depth'=4] {'depth'}, dimensions={0}, use_global_device_ids=true | all-gather | bytes 819200 | tf_op jit(solution)/shard_map/all_gather | solution.py:47
  173.9 0.0 copy-done.1
  173.9 0.0 copy-done.2
  173.9 4.1 %multiply_subtract_fusion = (f32[512,640]{1,0:T(8,128)}, f32[512,640]{1,0:T(8,128)}, f32[512,640]{1,0:T(8,128)}, bf16[512,640]{1,0:T(8,128)(2,1)}) fusion(f32[512,640]{1,0:T(8,128)S(1)} %copy-done.1, bf16[512,640]{1,0:T(8,128)(2,1)S(1)} %all_gather.11, f32[512,640]{1,0:T(8,128)S(1)} %copy-done.2, f32[512,640]{1,0:T(8,128)} %param.9), kind=kLoop, calls=%fused_computation.6 | loop fusion | flops 5570560 | bytes 9175040 | tf_op jit(solution)/shard_map/sub | solution.py:21
  178.0 0.0 all-gather.3.cloned.1.call-update
  178.0 0.0 reduce-scatter.3.cloned.1.call-start
  178.1 83.6 %all-gather.3.cloned.1.call-done = bf16[4096,640]{1,0:T(8,128)(2,1)} async-done(((bf16[512,640]{1,0:T(8,128)(2,1)}), bf16[4096,640]{1,0:T(8,128)(2,1)}) %all-gather.3.cloned.1.call-update) | async-done | bytes 5242896 | tf_op jit(solution)/shard_map/all_gather | solution.py:31
  261.7 7.6 %convolution_convert_fusion.1 = bf16[512,4096]{1,0:T(8,128)(2,1)} fusion(bf16[512,640]{1,0:T(8,128)(2,1)S(1)} %copy-done, bf16[4096,640]{1,0:T(8,128)(2,1)} %all-gather.3.cloned.1.call-done), kind=kOutput, calls=%fused_computation.1 | convolution fusion | flops 2686451712 | bytes 10092544 | tf_op jit(solution)/shard_map/dot_general | solution.py:29
  269.2 0.0 reduce-scatter.3.cloned.1.call-update
  269.3 55.3 %reduce-scatter.3.cloned.1.call-done = bf16[512,512]{1,0:T(8,128)(2,1)} async-done(((bf16[512,4096]{1,0:T(8,128)(2,1)}), bf16[512,512]{1,0:T(8,128)(2,1)}) %reduce-scatter.3.cloned.1.call-update) | async-done | bytes 524304 | tf_op jit(solution)/shard_map/reduce_scatter | solution.py:35
Async XLA Ops:
  7.2 60.4 %copy-start = (bf16[512,640]{1,0:T(8,128)(2,1)S(1)}, bf16[512,640]{1,0:T(8,128)(2,1)}, u32[]{:S(2)}) copy-start(bf16[512,640]{1,0:T(8,128)(2,1)} %param.6) | copy-start | bytes 1966084
  7.2 60.4 %all-gather.5.cloned.1.call-start = ((), (), s32[]{:S(2)}) async-start(), calls=%async_computation.4 | async-start | bytes 4718592 | tf_op jit(solution)/shard_map/all_gather | solution.py:38
  7.9 156.1 %reduce-scatter.5.cloned.1.call-start = ((), (), s32[]{:S(2)}) async-start(), calls=%async_computation.5 | async-start | bytes 5406720 | tf_op jit(solution)/shard_map/reduce_scatter | solution.py:39
  75.6 98.3 %copy-start.1 = (f32[512,640]{1,0:T(8,128)S(1)}, f32[512,640]{1,0:T(8,128)}, u32[]{:S(2)}) copy-start(f32[512,640]{1,0:T(8,128)} %param.7) | copy-start | bytes 3932164
  75.6 98.3 %copy-start.2 = (f32[512,640]{1,0:T(8,128)S(1)}, f32[512,640]{1,0:T(8,128)}, u32[]{:S(2)}) copy-start(f32[512,640]{1,0:T(8,128)} %param.8) | copy-start | bytes 3932164
  75.6 186.1 %all-gather.3.cloned.1.call-start = ((), (), s32[]{:S(2)}) async-start(), calls=%async_computation.2 | async-start | bytes 5898240 | tf_op jit(solution)/shard_map/all_gather | solution.py:31
  178.0 146.6 %reduce-scatter.3.cloned.1.call-start = ((), (), s32[]{:S(2)}) async-start(), calls=%async_computation.3 | async-start | bytes 4718592 | tf_op jit(solution)/shard_map/reduce_scatter | solution.py:35
Sparse Core Ops, SparseCore 0:
  9.8 57.7 all-gather.4
  75.7 88.2 reduce-scatter.4
  178.1 83.4 all-gather.2
  269.4 55.1 reduce-scatter.2
where the time goes:
time: 332 us; the launch traced here: 331 us
  waiting for transfers between devices  288 us (87%)
  matrix products  15.5 us (5%)
  between operations  13.8 us (4%)
  blocking collectives  9.88 us (3%)
  other arithmetic  4.11 us (1%)
    reduce_scatter x1, waiting for transfers between devices, on_device(): lax.psum_scatter(lax.dot_general(gathered, out_grad, (((0,), (0,)), ((),...  88.4 us
    all_gather x1, waiting for transfers between devices, on_device(): lax.all_gather(weight, 'row', axis=0, tiled=True)  83.6 us
    all_gather x1, waiting for transfers between devices, on_device(): gathered = lax.all_gather(context, 'col', axis=1, tiled=True)  59.6 us
    reduce_scatter x1, waiting for transfers between devices, on_device(): lax.psum_scatter(partial_terms.astype(jnp.bfloat16), 'col', scatter_dimen...  55.3 us
    all_gather x1, blocking collectives, on_device(): lax.all_gather(grad_share.astype(jnp.bfloat16), 'depth', axis=0, tiled=True)  9.88 us
    dot_general x1, matrix products, on_device(): lax.dot_general(gathered, out_grad, (((0,), (0,)), ((), ())), preferred_e...  7.96 us
    dot_general x1, matrix products, on_device(): lax.dot_general(out_grad, lax.all_gather(weight, 'row', axis=0, tiled=Tru...  7.56 us
  transfers between devices with their start and end apart: 4, of which 4 were waited for; matrix products, arithmetic and copies ran while one was open for 0% of the time, Pallas kernels for 0%

commit v1 on v0

v1 whole, which is shorter than its diff:
```python
import jax
import jax.numpy as jnp
from jax import lax
from jax.experimental import pallas as pl
from jax.experimental.pallas import tpu as pltpu
from jax.sharding import PartitionSpec as P

STEP = 10

beta_one = 0.9
beta_two = 0.95
adam_eps = 1e-08
learn_rate = 0.001
decay_rate = 0.1

MESH = pl.DeviceIdType.MESH
NZ = 8
U = 16


def adam_update(gradient, master, first_moment, second_moment):
    new_first = beta_one * first_moment + (1.0 - beta_one) * gradient
    new_second = beta_two * second_moment + (1.0 - beta_two) * gradient * gradient
    first_hat = new_first / (1.0 - beta_one**STEP)
    second_hat = new_second / (1.0 - beta_two**STEP)
    new_master = master - learn_rate * (
        first_hat / (jnp.sqrt(second_hat) + adam_eps) + decay_rate * master
    )
    return (new_master, new_first, new_second)


def mod(value, n):
    return lax.rem(value, jnp.int32(n))


def kernel(
    ctx_ref,
    og_ref,
    master_ref,
    ig_ref,
    grad_ref,
    og_all,
    ct_own,
    ct_sib,
    w16,
    w_in,
    w_pan,
    p_buf,
    r1,
    q_buf,
    r2,
    f_buf,
    gz,
    g_tile,
    g_sib,
    acc,
    ig_out,
    ig_in,
    z_send,
    z_recv,
    s_send,
    s_recv,
    m_send,
    m_recv,
    w_send,
    w_recv,
    r1_send,
    r1_recv,
    r2_send,
    r2_recv,
    h_send,
    h_recv,
    f_send,
    f_own_send,
    f_recv,
):
    row, z, dep = lax.axis_index("row"), lax.axis_index("col"), lax.axis_index("depth")
    x, yh = lax.div(row, jnp.int32(2)), mod(row, 2)
    yl, c = lax.div(dep, jnp.int32(2)), mod(dep, 2)
    y = yh * 2 + yl
    half = 16 * U
    tok = og_ref.shape[0]
    ht = tok // 2

    def z_peer(s):
        return (row, mod(z + s, NZ), dep)

    sibling = (row, z, yl * 2 + (1 - c))

    def x_peer(j):
        return (mod(x + j, 4) * 2 + yh, z, dep)

    def y_peer(j):
        yy = mod(y + j, 4)
        return (x * 2 + lax.div(yy, jnp.int32(2)), z, mod(yy, 2) * 2 + c)

    def remote(src, dst, send, recv, device):
        pltpu.make_async_remote_copy(
            src_ref=src,
            dst_ref=dst,
            send_sem=send,
            recv_sem=recv,
            device_id=device,
            device_id_type=MESH,
        ).start()

    def await_bytes(ref, sem):
        pltpu.make_async_copy(ref, ref, sem).wait()

    place = (
        pl.multiple_of(x * (4 * U) + y * U, U),
        pl.multiple_of(y * (4 * U) + x * U, U),
    )

    barrier = pltpu.get_barrier_semaphore()
    for s in range(1, NZ):
        pl.semaphore_signal(barrier, inc=1, device_id=z_peer(s), device_id_type=MESH)
    pl.semaphore_signal(barrier, inc=1, device_id=sibling, device_id_type=MESH)
    for j in range(8):
        for e in range(2):
            if j or e:
                pl.semaphore_signal(
                    barrier,
                    inc=1,
                    device_id=(mod(row + j, 8), z, mod(yl + e, 2) * 2 + c),
                    device_id_type=MESH,
                )
    w16[...] = master_ref[...].astype(jnp.bfloat16)
    ct_own[...] = ctx_ref[...].T
    pl.semaphore_wait(barrier, 23)

    def og(s, t):
        return og_ref if s == 0 and t == 0 else og_all.at[s, t]

    def part(ref, b):
        return ref.at[pl.ds(b * ht, ht)]

    def forward(s, b, d):
        if d == 0:
            to, peer = (s - 1) % NZ, z_peer(1)
        else:
            to, peer = (s + 1) % NZ, z_peer(NZ - 1)
        remote(
            part(og(s, 0), b), part(og_all.at[to, 0], b), z_send, z_recv.at[2 * to + b], peer
        )

    def to_sibling(s, b):
        remote(
            part(og(s, 0), b), part(og_all.at[s, 1], b), s_send, s_recv.at[s], sibling
        )

    def arrived(s, b):
        await_bytes(part(og_all.at[s, 0], b), z_recv.at[2 * s + b])

    forward(0, 0, 0)
    forward(0, 1, 1)
    forward(0, 1, 0)
    forward(0, 0, 1)

    ct_half = (1 - c) * half
    remote(
        ct_own.at[pl.ds(pl.multiple_of(ct_half, half), half)],
        ct_sib,
        m_send.at[0],
        m_recv.at[0],
        sibling,
    )
    to_sibling(0, 0)
    to_sibling(0, 1)

    odd = mod(z + row, 2)

    def w_place(row_to):
        xx, yy = lax.div(row_to, jnp.int32(2)), mod(row_to, 2) * 2 + yl
        a, b = xx + odd * (yy - xx), yy + odd * (xx - yy)
        return pl.ds(pl.multiple_of(c * half + a * (4 * U) + b * U, U), U)

    for j in range(1, 8):
        row_to = mod(row + j, 8)
        remote(
            w16.at[w_place(row_to)], w_in.at[row], w_send.at[0], w_recv.at[0], (row_to, z, dep)
        )
    w_in[row] = w16[w_place(row)]
    await_bytes(w_in.at[pl.ds(0, 7)], w_recv.at[0])

    for step in range(1, NZ):
        s = NZ - step
        remote(
            w_in.at[mod(z + step, NZ)],
            w_pan.at[s % 2, s // 2, pl.ds(place[s % 2], U)],
            w_send.at[1],
            w_recv.at[1],
            z_peer(step),
        )
    w_pan[0, 0, pl.ds(place[0], U)] = w_in[z]

    ct_mine = pl.ds(pl.multiple_of(c * half, half), half)

    def grad_partial(s):
        await_bytes(og_all.at[s, 1], s_recv.at[s])
        total = jnp.dot(ct_own[ct_mine, :], og(s, 0)[...], preferred_element_type=jnp.float32)
        total += jnp.dot(ct_sib[...], og_all[s, 1], preferred_element_type=jnp.float32)
        p_buf[s] = total.astype(jnp.bfloat16).reshape(4, 4 * U, total.shape[-1])
        axis, peer = (x, x_peer) if s % 2 == 0 else (y, y_peer)
        for j in range(1, 4):
            remote(
                p_buf.at[s, mod(axis + j, 4)],
                r1.at[s, j - 1],
                r1_send.at[s],
                r1_recv.at[s],
                peer(j),
            )

    def reduce_first(s):
        await_bytes(r1.at[s], r1_recv.at[s])
        axis = x if s % 2 == 0 else y
        total = p_buf[s, axis].astype(jnp.float32)
        for j in range(3):
            total += r1[s, j].astype(jnp.float32)
        q_buf[s] = total.astype(jnp.bfloat16).reshape(4, U, total.shape[-1])
        axis, peer = (y, y_peer) if s % 2 == 0 else (x, x_peer)
        for j in range(1, 4):
            remote(
                q_buf.at[s, mod(axis + j, 4)],
                r2.at[s, j - 1],
                r2_send.at[s],
                r2_recv.at[s],
                peer(j),
            )

    def reduce_second(s):
        await_bytes(r2.at[s], r2_recv.at[s])
        axis = y if s % 2 == 0 else x
        total = q_buf[s, axis].astype(jnp.float32)
        for j in range(3):
            total += r2[s, j].astype(jnp.float32)
        if s == 0:
            gz[0] = total.astype(jnp.bfloat16)
        else:
            f_buf[s] = total.astype(jnp.bfloat16)
            remote(f_buf.at[s], gz.at[s], h_send, h_recv.at[s], z_peer(s))

    def deliver(s):
        if s:
            await_bytes(gz.at[s], h_recv.at[s])
        row_to = mod(z + (NZ - s), NZ)
        spot = pl.ds(place[s % 2], U)
        remote(
            gz.at[s], g_tile.at[spot], f_send, f_recv, (row_to, z, (1 - yl) * 2 + c)
        )

        @pl.when(row_to != row)
        def _():
            remote(gz.at[s], g_tile.at[spot], f_own_send, f_recv, (row_to, z, dep))

        @pl.when(row_to == row)
        def _():
            g_tile[spot, :] = gz[s]

    def input_partial(s):
        w = w_pan[s % 2, s // 2]
        for t in range(2):
            term = lax.dot_general(
                og(s, t)[...], w, (((1,), (1,)), ((), ())), preferred_element_type=jnp.float32
            )
            if s == 0:
                acc[t] = term
            else:
                acc[t] += term

    await_bytes(ct_sib, m_recv.at[0])
    grad_partial(0)

    def w_gather(parity, axis_peer, rows, n, send, recv):
        view = w_pan.at[parity, :, rows]
        for j in range(1, 4):
            remote(view, view, send, recv, axis_peer(j))

    def w_gathered(parity, n, recv):
        await_bytes(w_pan.at[parity, :, pl.ds(0, 3 * n)], recv)

    await_bytes(w_in.at[pl.ds(0, 7)], w_recv.at[1])
    w_gather(0, y_peer, pl.ds(place[0], U), U, w_send.at[2], w_recv.at[2])
    w_gather(1, x_peer, pl.ds(place[1], U), U, w_send.at[3], w_recv.at[3])
    w_gathered(0, U, w_recv.at[2])
    w_gather(
        0, x_peer, pl.ds(pl.multiple_of(x * 4 * U, 4 * U), 4 * U), 4 * U, w_send.at[4], w_recv.at[4]
    )
    w_gathered(1, U, w_recv.at[3])
    w_gather(
        1, y_peer, pl.ds(pl.multiple_of(y * 4 * U, 4 * U), 4 * U), 4 * U, w_send.at[5], w_recv.at[5]
    )

    def pass_on(s_right, b_right, s_left, b_left, onward=True):
        arrived(s_right, b_right)
        if onward:
            forward(s_right, b_right, 0)
        to_sibling(s_right, b_right)
        arrived(s_left, b_left)
        if onward:
            forward(s_left, b_left, 1)
        to_sibling(s_left, b_left)

    pass_on(7, 0, 1, 1)
    reduce_first(0)
    w_gathered(0, 4 * U, w_recv.at[4])
    input_partial(0)
    reduce_second(0)
    deliver(0)
    w_gathered(1, 4 * U, w_recv.at[5])

    pass_on(7, 1, 1, 0)
    grad_partial(7)
    grad_partial(1)
    pass_on(6, 0, 2, 1)
    reduce_first(7)
    reduce_first(1)
    input_partial(7)
    reduce_second(7)
    reduce_second(1)
    pass_on(6, 1, 2, 0)
    grad_partial(6)
    grad_partial(2)
    deliver(7)
    deliver(1)
    pass_on(5, 0, 3, 1)
    reduce_first(6)
    reduce_first(2)
    input_partial(1)
    reduce_second(6)
    reduce_second(2)
    input_partial(6)
    pass_on(5, 1, 3, 0, onward=False)
    grad_partial(5)
    grad_partial(3)
    deliver(6)
    deliver(2)
    input_partial(2)
    reduce_first(5)
    reduce_first(3)
    input_partial(5)
    reduce_second(5)
    reduce_second(3)
    input_partial(3)
    deliver(5)
    deliver(3)
    arrived(4, 0)
    to_sibling(4, 0)
    arrived(4, 1)
    to_sibling(4, 1)
    grad_partial(4)
    input_partial(4)
    ig_out[...] = acc[1].astype(jnp.bfloat16)
    remote(ig_out, ig_in, m_send.at[1], m_recv.at[1], sibling)
    reduce_first(4)
    ig_ref[:, ct_mine] = acc[0].astype(jnp.bfloat16)
    reduce_second(4)
    await_bytes(ig_in, m_recv.at[1])
    ig_ref[:, pl.ds(pl.multiple_of(ct_half, half), half)] = ig_in[...]
    deliver(4)

    await_bytes(g_tile.at[pl.ds(0, 15 * U)], f_recv)
    remote(g_tile, g_sib, m_send.at[2], m_recv.at[2], sibling)
    grad_ref[ct_mine, :] = g_tile[...]
    await_bytes(g_sib, m_recv.at[2])
    grad_ref[pl.ds(pl.multiple_of(ct_half, half), half), :] = g_sib[...]

    await_bytes(og_all.at[pl.ds(0, 7), 0], z_send)
    await_bytes(og_all.at[:, 1], s_send)
    await_bytes(ct_sib, m_send.at[0])
    await_bytes(ig_in, m_send.at[1])
    await_bytes(g_sib, m_send.at[2])
    await_bytes(w_in.at[pl.ds(0, 7)], w_send.at[0])
    await_bytes(w_in.at[pl.ds(0, 7)], w_send.at[1])
    w_gathered(0, U, w_send.at[2])
    w_gathered(1, U, w_send.at[3])
    w_gathered(0, 4 * U, w_send.at[4])
    w_gathered(1, 4 * U, w_send.at[5])
    for s in range(NZ):
        await_bytes(r1.at[s], r1_send.at[s])
        await_bytes(r2.at[s], r2_send.at[s])
    await_bytes(f_buf.at[pl.ds(0, 7)], h_send)
    await_bytes(gz, f_send)
    await_bytes(gz.at[pl.ds(0, 7)], f_own_send)


def on_device(context, out_grad, master, first_moment, second_moment):
    tok, width = out_grad.shape
    bf16 = jnp.bfloat16
    half = 16 * U
    dma = pltpu.SemaphoreType.DMA
    vmem = pl.BlockSpec(memory_space=pltpu.VMEM)
    input_grad, gradient = pl.pallas_call(
        kernel,
        out_shape=(
            jax.ShapeDtypeStruct((tok, 2 * half), bf16),
            jax.ShapeDtypeStruct((2 * half, width), bf16),
        ),
        in_specs=[vmem] * 3,
        out_specs=(vmem, vmem),
        scratch_shapes=[
            pltpu.VMEM((NZ, 2, tok, width), bf16),
            pltpu.VMEM((2 * half, tok), bf16),
            pltpu.VMEM((half, tok), bf16),
            pltpu.VMEM((2 * half, width), bf16),
            pltpu.VMEM((8, U, width), bf16),
            pltpu.VMEM((2, NZ // 2, half, width), bf16),
            pltpu.VMEM((NZ, 4, 4 * U, width), bf16),
            pltpu.VMEM((NZ, 3, 4 * U, width), bf16),
            pltpu.VMEM((NZ, 4, U, width), bf16),
            pltpu.VMEM((NZ, 3, U, width), bf16),
            pltpu.VMEM((NZ, U, width), bf16),
            pltpu.VMEM((NZ, U, width), bf16),
            pltpu.VMEM((half, width), bf16),
            pltpu.VMEM((half, width), bf16),
            pltpu.VMEM((2, tok, half), jnp.float32),
            pltpu.VMEM((tok, half), bf16),
            pltpu.VMEM((tok, half), bf16),
            dma,
            dma((2 * NZ,)),
            dma,
            dma((NZ,)),
            dma((3,)),
            dma((3,)),
            dma((6,)),
            dma((6,)),
            dma((NZ,)),
            dma((NZ,)),
            dma((NZ,)),
            dma((NZ,)),
            dma,
            dma((NZ,)),
            dma,
            dma,
            dma,
        ],
        compiler_params=pltpu.CompilerParams(
            collective_id=0, has_side_effects=True, vmem_limit_bytes=50 * 1024 * 1024
        ),
        cost_estimate=pl.CostEstimate(
            flops=8 * tok * width * 2 * half * 2, bytes_accessed=4_000_000, transcendentals=0
        ),
    )(context, out_grad, master)
    new_master, new_first, new_second = adam_update(
        gradient.astype(jnp.float32), master, first_moment, second_moment
    )
    return (input_grad, new_master, new_first, new_second)


def solution(mesh):
    in_specs = (
        P(("row", "depth"), "col"),
        P(("row", "depth"), "col"),
        P("row", "col"),
        P("row", "col"),
        P("row", "col"),
    )
    out_specs = (P(("row", "depth"), "col"), P("row", "col"), P("row", "col"), P("row", "col"))
    return jax.shard_map(
        on_device, mesh=mesh, in_specs=in_specs, out_specs=out_specs, check_vma=False
    )
```

time: 332 us -> 132 us (0.40)
  waiting for transfers between devices: 288 us -> 0 us
  Pallas kernels: 0 us -> 123 us
  matrix products: 15.5 us -> 0 us
  between operations: 13.8 us -> 0.67 us
  blocking collectives: 9.88 us -> 0 us
  local copies, waits for them, and re-layouts: 0.02 us -> 4.24 us
    reduce_scatter x2 -> x0, waiting for transfers between devices: 144 us -> none  [the longest x1 88.4 us: on_device(): lax.psum_scatter(lax.dot_general(gathered, out_grad, (((0,), (0,)), ((),...]
    all_gather x2 -> x0, waiting for transfers between devices: 143 us -> none  [the longest x1 83.6 us: on_device(): lax.all_gather(weight, 'row', axis=0, tiled=True)]
    pallas_call x0 -> x1, Pallas kernels: none -> 123 us  [on_device(): pl.pallas_call(kernel, out_shape=(jax.ShapeDtypeStruct((tok, 2 * half), b...]
    dot_general x2 -> x0, matrix products: 15.5 us -> none  [the longest x1 7.96 us: on_device(): lax.dot_general(gathered, out_grad, (((0,), (0,)), ((), ())), preferred_e...]
    all_gather x1 -> x0, blocking collectives: 9.88 us -> none  [on_device(): lax.all_gather(grad_share.astype(jnp.bfloat16), 'depth', axis=0, tiled=True)]
    unnamed x6 -> x11, local copies, waits for them, and re-layouts: 0.02 us -> 4.24 us
  transfers between devices with their start and end apart: 4 -> 0, of which waited for: 4 -> 0; matrix products, arithmetic and copies ran while one was open for 0% -> 0% of each run, Pallas kernels for 0% -> 0%
where the time goes in v1:
time: 132 us; the launch traced here: 131 us
  Pallas kernels  123 us (93%)
  local copies, waits for them, and re-layouts  4.24 us (3%)
  other arithmetic  2.58 us (2%)
    pallas_call x1, Pallas kernels, on_device(): pl.pallas_call(kernel, out_shape=(jax.ShapeDtypeStruct((tok, 2 * half), b...  123 us
    unnamed x11, local copies, waits for them, and re-layouts  4.24 us

profile of v1, /device:TPU:5, one launch (start us, length us, event | category | flops | bytes accessed | tf_op | source)
XLA Modules:
  0.0 130.8 jit_solution(4369477568373246485)
XLA Ops:
  0.6 0.0 copy-start
  0.6 1.3 copy-done
  1.9 0.0 copy-start.1
  2.0 1.1 copy-done.1
  3.0 0.0 copy-start.2
  3.0 1.0 copy-done.2
  4.1 0.0 copy-start.3
  4.1 0.0 copy-start.4
  4.1 123.3 %shard_map.84 = (bf16[512,512]{1,0:T(8,128)(2,1)S(1)}, bf16[512,640]{1,0:T(8,128)(2,1)S(1)}) custom-call(bf16[512,512]{1,0:T(8,128)(2,1)S(1)} %copy-done.2, bf16[512,640]{1,0:T(8,128)(2,1)S(1)} %copy-done.1, f32[512,640]{1,0:T(8,128)S(1)} %copy-done), custom_call_target="tpu_custom_call" | custom-call | flops 2684354560 | bytes 4000000 | tf_op jit(solution)/shard_map/pallas_call | solution.py:393
  127.4 0.0 copy-done.3
  127.4 0.0 copy-done.4
  127.4 2.6 %multiply_subtract_fusion = (f32[512,640]{1,0:T(8,128)}, f32[512,640]{1,0:T(8,128)}, f32[512,640]{1,0:T(8,128)}) fusion(f32[512,640]{1,0:T(8,128)S(1)} %copy-done, bf16[512,640]{1,0:T(8,128)(2,1)S(1)} %get-tuple-element.7, f32[512,640]{1,0:T(8,128)S(1)} %copy-done.3, f32[512,640]{1,0:T(8,128)S(1)} %copy-done.4), kind=kLoop, calls=%fused_computation.4 | loop fusion | flops 5242880 | bytes 8519680 | tf_op jit(solution)/shard_map/sub | solution.py:26
  130.0 0.8 copy.10
Async XLA Ops:
  0.6 1.3 %copy-start = (f32[512,640]{1,0:T(8,128)S(1)}, f32[512,640]{1,0:T(8,128)}, u32[]{:S(2)}) copy-start(f32[512,640]{1,0:T(8,128)} %master_ref.1) | copy-start | bytes 3932164
  1.9 1.1 copy-start.1
  3.0 1.0 copy-start.2
  4.1 123.3 %copy-start.3 = (f32[512,640]{1,0:T(8,128)S(1)}, f32[512,640]{1,0:T(8,128)}, u32[]{:S(2)}) copy-start(f32[512,640]{1,0:T(8,128)} %param.8) | copy-start | bytes 3932164
  4.1 123.3 %copy-start.4 = (f32[512,640]{1,0:T(8,128)S(1)}, f32[512,640]{1,0:T(8,128)}, u32[]{:S(2)}) copy-start(f32[512,640]{1,0:T(8,128)} %param.9) | copy-start | bytes 3932164

commit v2 on v1

--- a/solution.py
+++ b/solution.py
@@ -39,6 +39,8 @@
     master_ref,
     ig_ref,
     grad_ref,
+    ctx_v,
+    master_v,
     og_all,
     ct_own,
     ct_sib,
@@ -49,6 +51,7 @@
     r1,
     q_buf,
     r2,
+    rd,
     f_buf,
     gz,
     g_tile,
@@ -73,6 +76,7 @@
     f_send,
     f_own_send,
     f_recv,
+    l_sem,
 ):
     row, z, dep = lax.axis_index("row"), lax.axis_index("col"), lax.axis_index("depth")
     x, yh = lax.div(row, jnp.int32(2)), mod(row, 2)
@@ -125,12 +129,20 @@
                     device_id=(mod(row + j, 8), z, mod(yl + e, 2) * 2 + c),
                     device_id_type=MESH,
                 )
-    w16[...] = master_ref[...].astype(jnp.bfloat16)
-    ct_own[...] = ctx_ref[...].T
+    pltpu.make_async_copy(master_ref, master_v, l_sem.at[0]).start()
+    pltpu.make_async_copy(ctx_ref, ctx_v, l_sem.at[1]).start()
+    pltpu.make_async_copy(og_ref, og_all.at[0, 0], l_sem.at[2]).start()
+    await_bytes(master_v, l_sem.at[0])
+    w16[...] = master_v[...].astype(jnp.bfloat16)
+    await_bytes(ctx_v, l_sem.at[1])
+    ct_own[...] = ctx_v[...].T
     pl.semaphore_wait(barrier, 23)
 
     def og(s, t):
-        return og_ref if s == 0 and t == 0 else og_all.at[s, t]
+        return og_all.at[s, t]
+
+    def source(s):
+        return og_ref if s == 0 else og_all.at[s, 0]
 
     def part(ref, b):
         return ref.at[pl.ds(b * ht, ht)]
@@ -141,22 +153,32 @@
         else:
             to, peer = (s + 1) % NZ, z_peer(NZ - 1)
         remote(
-            part(og(s, 0), b), part(og_all.at[to, 0], b), z_send, z_recv.at[2 * to + b], peer
+            part(source(s), b), part(og_all.at[to, 0], b), z_send, z_recv.at[2 * to + b], peer
         )
 
     def to_sibling(s, b):
         remote(
-            part(og(s, 0), b), part(og_all.at[s, 1], b), s_send, s_recv.at[s], sibling
+            part(source(s), b), part(og_all.at[s, 1], b), s_send, s_recv.at[s], sibling
         )
 
     def arrived(s, b):
         await_bytes(part(og_all.at[s, 0], b), z_recv.at[2 * s + b])
 
+    late = lax.div(mod(z + NZ - row, NZ), jnp.int32(4))
+
+    def w_place(row_to):
+        xx, yy = lax.div(row_to, jnp.int32(2)), mod(row_to, 2) * 2 + yl
+        a, b = xx + late * (yy - xx), yy + late * (xx - yy)
+        return pl.ds(pl.multiple_of(c * half + a * (4 * U) + b * U, U), U)
+
+    for j in range(1, 8):
+        row_to = mod(row + j, 8)
+        remote(
+            w16.at[w_place(row_to)], w_in.at[row], w_send.at[0], w_recv.at[0], (row_to, z, dep)
+        )
+    w_in[row] = w16[w_place(row)]
     forward(0, 0, 0)
     forward(0, 1, 1)
-    forward(0, 1, 0)
-    forward(0, 0, 1)
-
     ct_half = (1 - c) * half
     remote(
         ct_own.at[pl.ds(pl.multiple_of(ct_half, half), half)],
@@ -165,29 +187,17 @@
         m_recv.at[0],
         sibling,
     )
+
     to_sibling(0, 0)
     to_sibling(0, 1)
 
-    odd = mod(z + row, 2)
-
-    def w_place(row_to):
-        xx, yy = lax.div(row_to, jnp.int32(2)), mod(row_to, 2) * 2 + yl
-        a, b = xx + odd * (yy - xx), yy + odd * (xx - yy)
-        return pl.ds(pl.multiple_of(c * half + a * (4 * U) + b * U, U), U)
-
-    for j in range(1, 8):
-        row_to = mod(row + j, 8)
-        remote(
-            w16.at[w_place(row_to)], w_in.at[row], w_send.at[0], w_recv.at[0], (row_to, z, dep)
-        )
-    w_in[row] = w16[w_place(row)]
     await_bytes(w_in.at[pl.ds(0, 7)], w_recv.at[0])
 
     for step in range(1, NZ):
         s = NZ - step
         remote(
             w_in.at[mod(z + step, NZ)],
-            w_pan.at[s % 2, s // 2, pl.ds(place[s % 2], U)],
+            w_pan.at[s // 4, s % 4, pl.ds(place[s // 4], U)],
             w_send.at[1],
             w_recv.at[1],
             z_peer(step),
@@ -196,12 +206,15 @@
 
     ct_mine = pl.ds(pl.multiple_of(c * half, half), half)
 
+    def grad_terms(s):
+        total = jnp.dot(ct_own[ct_mine, :], og(s, 0)[...], preferred_element_type=jnp.float32)
+        total += jnp.dot(ct_sib[...], og_all[s, 1], preferred_element_type=jnp.float32)
+        return total.astype(jnp.bfloat16).reshape(4, 4 * U, total.shape[-1])
+
     def grad_partial(s):
         await_bytes(og_all.at[s, 1], s_recv.at[s])
-        total = jnp.dot(ct_own[ct_mine, :], og(s, 0)[...], preferred_element_type=jnp.float32)
-        total += jnp.dot(ct_sib[...], og_all[s, 1], preferred_element_type=jnp.float32)
-        p_buf[s] = total.astype(jnp.bfloat16).reshape(4, 4 * U, total.shape[-1])
-        axis, peer = (x, x_peer) if s % 2 == 0 else (y, y_peer)
+        p_buf[s] = grad_terms(s)
+        axis, peer = (x, x_peer) if s < 4 else (y, y_peer)
         for j in range(1, 4):
             remote(
                 p_buf.at[s, mod(axis + j, 4)],
@@ -213,12 +226,12 @@
 
     def reduce_first(s):
         await_bytes(r1.at[s], r1_recv.at[s])
-        axis = x if s % 2 == 0 else y
+        axis = x if s < 4 else y
         total = p_buf[s, axis].astype(jnp.float32)
         for j in range(3):
             total += r1[s, j].astype(jnp.float32)
         q_buf[s] = total.astype(jnp.bfloat16).reshape(4, U, total.shape[-1])
-        axis, peer = (y, y_peer) if s % 2 == 0 else (x, x_peer)
+        axis, peer = (y, y_peer) if s < 4 else (x, x_peer)
         for j in range(1, 4):
             remote(
                 q_buf.at[s, mod(axis + j, 4)],
@@ -230,7 +243,7 @@
 
     def reduce_second(s):
         await_bytes(r2.at[s], r2_recv.at[s])
-        axis = y if s % 2 == 0 else x
+        axis = y if s < 4 else x
         total = q_buf[s, axis].astype(jnp.float32)
         for j in range(3):
             total += r2[s, j].astype(jnp.float32)
@@ -240,11 +253,34 @@
             f_buf[s] = total.astype(jnp.bfloat16)
             remote(f_buf.at[s], gz.at[s], h_send, h_recv.at[s], z_peer(s))
 
+    def grad_last():
+        await_bytes(og_all.at[4, 1], s_recv.at[4])
+        p_buf[4] = grad_terms(4)
+        for jx in range(4):
+            for jy in range(4):
+                if jx or jy:
+                    xx, yy = mod(x + jx, 4), mod(y + jy, 4)
+                    remote(
+                        p_buf.at[4, yy, pl.ds(pl.multiple_of(xx * U, U), U)],
+                        rd.at[jx * 4 + jy - 1],
+                        r1_send.at[4],
+                        r1_recv.at[4],
+                        (xx * 2 + lax.div(yy, jnp.int32(2)), z, mod(yy, 2) * 2 + c),
+                    )
+
+    def reduce_last():
+        await_bytes(rd, r1_recv.at[4])
+        total = p_buf[4, y, pl.ds(pl.multiple_of(x * U, U), U)].astype(jnp.float32)
+        for j in range(15):
+            total += rd[j].astype(jnp.float32)
+        f_buf[4] = total.astype(jnp.bfloat16)
+        remote(f_buf.at[4], gz.at[4], h_send, h_recv.at[4], z_peer(4))
+
     def deliver(s):
         if s:
             await_bytes(gz.at[s], h_recv.at[s])
         row_to = mod(z + (NZ - s), NZ)
-        spot = pl.ds(place[s % 2], U)
+        spot = pl.ds(place[s // 4], U)
         remote(
             gz.at[s], g_tile.at[spot], f_send, f_recv, (row_to, z, (1 - yl) * 2 + c)
         )
@@ -258,7 +294,7 @@
             g_tile[spot, :] = gz[s]
 
     def input_partial(s):
-        w = w_pan[s % 2, s // 2]
+        w = w_pan[s // 4, s % 4]
         for t in range(2):
             term = lax.dot_general(
                 og(s, t)[...], w, (((1,), (1,)), ((), ())), preferred_element_type=jnp.float32
@@ -268,9 +304,6 @@
             else:
                 acc[t] += term
 
-    await_bytes(ct_sib, m_recv.at[0])
-    grad_partial(0)
-
     def w_gather(parity, axis_peer, rows, n, send, recv):
         view = w_pan.at[parity, :, rows]
         for j in range(1, 4):
@@ -279,91 +312,93 @@
     def w_gathered(parity, n, recv):
         await_bytes(w_pan.at[parity, :, pl.ds(0, 3 * n)], recv)
 
+    def pass_on(s, b, d, onward=True):
+        arrived(s, b)
+        if onward:
+            forward(s, b, d)
+        to_sibling(s, b)
+
+    rows_x = pl.ds(pl.multiple_of(x * 4 * U, 4 * U), 4 * U)
+    rows_y = pl.ds(pl.multiple_of(y * 4 * U, 4 * U), 4 * U)
+
     await_bytes(w_in.at[pl.ds(0, 7)], w_recv.at[1])
+    forward(0, 1, 0)
+    forward(0, 0, 1)
     w_gather(0, y_peer, pl.ds(place[0], U), U, w_send.at[2], w_recv.at[2])
     w_gather(1, x_peer, pl.ds(place[1], U), U, w_send.at[3], w_recv.at[3])
+    await_bytes(og_all.at[0, 0], l_sem.at[2])
+    await_bytes(ct_sib, m_recv.at[0])
+    pass_on(7, 0, 0)
+    pass_on(1, 1, 1)
+    grad_partial(0)
     w_gathered(0, U, w_recv.at[2])
-    w_gather(
-        0, x_peer, pl.ds(pl.multiple_of(x * 4 * U, 4 * U), 4 * U), 4 * U, w_send.at[4], w_recv.at[4]
-    )
+    w_gather(0, x_peer, rows_x, 4 * U, w_send.at[4], w_recv.at[4])
     w_gathered(1, U, w_recv.at[3])
-    w_gather(
-        1, y_peer, pl.ds(pl.multiple_of(y * 4 * U, 4 * U), 4 * U), 4 * U, w_send.at[5], w_recv.at[5]
-    )
-
-    def pass_on(s_right, b_right, s_left, b_left, onward=True):
-        arrived(s_right, b_right)
-        if onward:
-            forward(s_right, b_right, 0)
-        to_sibling(s_right, b_right)
-        arrived(s_left, b_left)
-        if onward:
-            forward(s_left, b_left, 1)
-        to_sibling(s_left, b_left)
-
-    pass_on(7, 0, 1, 1)
+    w_gather(1, y_peer, rows_y, 4 * U, w_send.at[5], w_recv.at[5])
+    pass_on(7, 1, 0)
+    pass_on(1, 0, 1)
+    grad_partial(7)
+    grad_partial(1)
     reduce_first(0)
+    pass_on(6, 0, 0)
+    pass_on(2, 1, 1)
+    pass_on(6, 1, 0)
+    pass_on(2, 0, 1)
+    reduce_first(7)
+    reduce_first(1)
+    grad_partial(6)
+    grad_partial(2)
+    reduce_second(0)
+    reduce_second(7)
+    reduce_second(1)
+    pass_on(5, 0, 0)
+    pass_on(3, 1, 1)
+    pass_on(5, 1, 0, onward=False)
+    pass_on(3, 0, 1, onward=False)
+    reduce_first(6)
+    reduce_first(2)
+    grad_partial(5)
+    grad_partial(3)
+    deliver(0)
+    deliver(7)
+    deliver(1)
     w_gathered(0, 4 * U, w_recv.at[4])
     input_partial(0)
-    reduce_second(0)
-    deliver(0)
+    input_partial(1)
     w_gathered(1, 4 * U, w_recv.at[5])
-
-    pass_on(7, 1, 1, 0)
-    grad_partial(7)
-    grad_partial(1)
-    pass_on(6, 0, 2, 1)
-    reduce_first(7)
-    reduce_first(1)
     input_partial(7)
-    reduce_second(7)
-    reduce_second(1)
-    pass_on(6, 1, 2, 0)
-    grad_partial(6)
-    grad_partial(2)
-    deliver(7)
-    deliver(1)
-    pass_on(5, 0, 3, 1)
-    reduce_first(6)
-    reduce_first(2)
-    input_partial(1)
     reduce_second(6)
     reduce_second(2)
-    input_partial(6)
-    pass_on(5, 1, 3, 0, onward=False)
-    grad_partial(5)
-    grad_partial(3)
+    pass_on(4, 0, 0, onward=False)
+    pass_on(4, 1, 1, onward=False)
+    reduce_first(5)
+    reduce_first(3)
+    grad_last()
     deliver(6)
     deliver(2)
-    input_partial(2)
-    reduce_first(5)
-    reduce_first(3)
-    input_partial(5)
     reduce_second(5)
     reduce_second(3)
+    input_partial(2)
+    input_partial(6)
+    input_partial(5)
     input_partial(3)
+    reduce_last()
     deliver(5)
     deliver(3)
-    arrived(4, 0)
-    to_sibling(4, 0)
-    arrived(4, 1)
-    to_sibling(4, 1)
-    grad_partial(4)
     input_partial(4)
     ig_out[...] = acc[1].astype(jnp.bfloat16)
     remote(ig_out, ig_in, m_send.at[1], m_recv.at[1], sibling)
-    reduce_first(4)
+    deliver(4)
     ig_ref[:, ct_mine] = acc[0].astype(jnp.bfloat16)
-    reduce_second(4)
-    await_bytes(ig_in, m_recv.at[1])
-    ig_ref[:, pl.ds(pl.multiple_of(ct_half, half), half)] = ig_in[...]
-    deliver(4)
+    ct_other = pl.ds(pl.multiple_of(ct_half, half), half)
 
     await_bytes(g_tile.at[pl.ds(0, 15 * U)], f_recv)
     remote(g_tile, g_sib, m_send.at[2], m_recv.at[2], sibling)
     grad_ref[ct_mine, :] = g_tile[...]
+    await_bytes(ig_in, m_recv.at[1])
+    ig_ref[:, ct_other] = ig_in[...]
     await_bytes(g_sib, m_recv.at[2])
-    grad_ref[pl.ds(pl.multiple_of(ct_half, half), half), :] = g_sib[...]
+    grad_ref[ct_other, :] = g_sib[...]
 
     await_bytes(og_all.at[pl.ds(0, 7), 0], z_send)
     await_bytes(og_all.at[:, 1], s_send)
@@ -377,8 +412,11 @@
     w_gathered(0, 4 * U, w_send.at[4])
     w_gathered(1, 4 * U, w_send.at[5])
     for s in range(NZ):
-        await_bytes(r1.at[s], r1_send.at[s])
-        await_bytes(r2.at[s], r2_send.at[s])
+        if s == 4:
+            await_bytes(rd, r1_send.at[s])
+        else:
+            await_bytes(r1.at[s], r1_send.at[s])
+            await_bytes(r2.at[s], r2_send.at[s])
     await_bytes(f_buf.at[pl.ds(0, 7)], h_send)
     await_bytes(gz, f_send)
     await_bytes(gz.at[pl.ds(0, 7)], f_own_send)
@@ -396,9 +434,11 @@
             jax.ShapeDtypeStruct((tok, 2 * half), bf16),
             jax.ShapeDtypeStruct((2 * half, width), bf16),
         ),
-        in_specs=[vmem] * 3,
+        in_specs=[pl.BlockSpec(memory_space=pltpu.HBM)] * 3,
         out_specs=(vmem, vmem),
         scratch_shapes=[
+            pltpu.VMEM((tok, 2 * half), bf16),
+            pltpu.VMEM((2 * half, width), jnp.float32),
             pltpu.VMEM((NZ, 2, tok, width), bf16),
             pltpu.VMEM((2 * half, tok), bf16),
             pltpu.VMEM((half, tok), bf16),
@@ -409,6 +449,7 @@
             pltpu.VMEM((NZ, 3, 4 * U, width), bf16),
             pltpu.VMEM((NZ, 4, U, width), bf16),
             pltpu.VMEM((NZ, 3, U, width), bf16),
+            pltpu.VMEM((15, U, width), bf16),
             pltpu.VMEM((NZ, U, width), bf16),
             pltpu.VMEM((NZ, U, width), bf16),
             pltpu.VMEM((half, width), bf16),
@@ -433,9 +474,10 @@
             dma,
             dma,
             dma,
+            dma((3,)),
         ],
         compiler_params=pltpu.CompilerParams(
-            collective_id=0, has_side_effects=True, vmem_limit_bytes=50 * 1024 * 1024
+            collective_id=0, has_side_effects=True, vmem_limit_bytes=60 * 1024 * 1024
         ),
         cost_estimate=pl.CostEstimate(
             flops=8 * tok * width * 2 * half * 2, bytes_accessed=4_000_000, transcendentals=0

time: 132 us -> 97 us (0.73)
  Pallas kernels: 123 us -> 91.7 us
  local copies, waits for them, and re-layouts: 4.24 us -> 0.81 us
    pallas_call x1, Pallas kernels: 123 us -> 91.7 us  [on_device(): pl.pallas_call(kernel, out_shape=(jax.ShapeDtypeStruct((tok, 2 * half), b...]
    unnamed x11 -> x9, local copies, waits for them, and re-layouts: 4.24 us -> 0.81 us
where the time goes in v2:
time: 97 us; the launch traced here: 96.9 us
  Pallas kernels  91.7 us (95%)
  other arithmetic  3.7 us (4%)
    pallas_call x1, Pallas kernels, on_device(): pl.pallas_call(kernel, out_shape=(jax.ShapeDtypeStruct((tok, 2 * half), b...  91.7 us
    sub x1, other arithmetic, adam_update(): master - learn_rate * (first_hat / (jnp.sqrt(second_hat) + adam_eps) + de...  3.7 us

profile of v2, /device:TPU:5, one launch (start us, length us, event | category | flops | bytes accessed | tf_op | source)
XLA Modules:
  0.0 96.9 jit_solution(11457709689047972825)
XLA Ops:
  0.6 0.0 copy-start
  0.6 0.0 copy-start.2
  0.7 0.0 copy-start.1
  0.7 91.7 %shard_map.84 = (bf16[512,512]{1,0:T(8,128)(2,1)}, bf16[512,640]{1,0:T(8,128)(2,1)}) custom-call(bf16[512,512]{1,0:T(8,128)(2,1)} %ctx_ref.1, bf16[512,640]{1,0:T(8,128)(2,1)} %og_ref.1, f32[512,640]{1,0:T(8,128)} %master_ref.1), custom_call_target="tpu_custom_call" | custom-call | flops 2684354560 | bytes 4000000 | tf_op jit(solution)/shard_map/pallas_call | solution.py:431
  92.3 0.0 copy-done
  92.4 0.0 copy-done.2
  92.4 0.0 copy-done.1
  92.4 0.0 copy-start.3
  92.4 3.7 %multiply_subtract_fusion = (f32[512,640]{1,0:T(8,128)}, f32[512,640]{1,0:T(8,128)}, f32[512,640]{1,0:T(8,128)}) fusion(f32[512,640]{1,0:T(8,128)S(1)} %copy-done, bf16[512,640]{1,0:T(8,128)(2,1)} %get-tuple-element.7, f32[512,640]{1,0:T(8,128)S(1)} %copy-done.1, f32[512,640]{1,0:T(8,128)S(1)} %copy-done.2), kind=kLoop, calls=%fused_computation.4 | loop fusion | flops 5242880 | bytes 8519680 | tf_op jit(solution)/shard_map/sub | solution.py:26
  96.1 0.0 copy-done.3
  96.1 0.8 copy.10
Async XLA Ops:
  0.6 91.7 %copy-start = (f32[512,640]{1,0:T(8,128)S(1)}, f32[512,640]{1,0:T(8,128)}, u32[]{:S(2)}) copy-start(f32[512,640]{1,0:T(8,128)} %master_ref.1) | copy-start | bytes 3932164
  0.6 91.7 %copy-start.2 = (f32[512,640]{1,0:T(8,128)S(1)}, f32[512,640]{1,0:T(8,128)}, u32[]{:S(2)}) copy-start(f32[512,640]{1,0:T(8,128)} %param.9) | copy-start | bytes 3932164
  0.7 91.7 %copy-start.1 = (f32[512,640]{1,0:T(8,128)S(1)}, f32[512,640]{1,0:T(8,128)}, u32[]{:S(2)}) copy-start(f32[512,640]{1,0:T(8,128)} %param.8) | copy-start | bytes 3932164
  92.4 3.7 %copy-start.3 = (bf16[512,512]{1,0:T(8,128)(2,1)S(1)}, bf16[512,512]{1,0:T(8,128)(2,1)}, u32[]{:S(2)}) copy-start(bf16[512,512]{1,0:T(8,128)(2,1)} %get-tuple-element.15) | copy-start | bytes 1572868

commit v3 on v2

--- a/solution.py
+++ b/solution.py
@@ -15,14 +15,15 @@
 
 MESH = pl.DeviceIdType.MESH
 NZ = 8
+CUT = 256
 U = 16
 
 
 def adam_update(gradient, master, first_moment, second_moment):
     new_first = beta_one * first_moment + (1.0 - beta_one) * gradient
     new_second = beta_two * second_moment + (1.0 - beta_two) * gradient * gradient
-    first_hat = new_first / (1.0 - beta_one**STEP)
-    second_hat = new_second / (1.0 - beta_two**STEP)
+    first_hat = new_first * (1.0 / (1.0 - beta_one**STEP))
+    second_hat = new_second * (1.0 / (1.0 - beta_two**STEP))
     new_master = master - learn_rate * (
         first_hat / (jnp.sqrt(second_hat) + adam_eps) + decay_rate * master
     )
@@ -132,37 +133,46 @@
     pltpu.make_async_copy(master_ref, master_v, l_sem.at[0]).start()
     pltpu.make_async_copy(ctx_ref, ctx_v, l_sem.at[1]).start()
     pltpu.make_async_copy(og_ref, og_all.at[0, 0], l_sem.at[2]).start()
+    pl.semaphore_wait(barrier, 23)
+
+    def og(s, t):
+        return og_all.at[s, t]
+
+    def source(s):
+        return og_ref if s == 0 else og_all.at[s, 0]
+
+    cols = (pl.ds(0, CUT), pl.ds(CUT, og_ref.shape[1] - CUT))
+
+    def part(ref, b, d=None):
+        return ref.at[:, cols[b]] if d is None else ref.at[pl.ds(d * ht, ht), cols[b]]
+
+    def token_half(s, d):
+        return d if s == 4 else None
+
+    def forward(s, b, d):
+        to, peer = ((s - 1) % NZ, z_peer(1)) if d == 0 else (s + 1, z_peer(NZ - 1))
+        h = token_half(to, d)
+        remote(
+            part(source(s), b, h),
+            part(og_all.at[to, 0], b, h),
+            z_send,
+            z_recv.at[d, to, b],
+            peer,
+        )
+
+    def to_sibling(s, b, d=0):
+        h = token_half(s, d)
+        remote(
+            part(source(s), b, h), part(og_all.at[s, 1], b, h), s_send, s_recv.at[s, b], sibling
+        )
+
+    def arrived(s, b, d):
+        await_bytes(part(og_all.at[s, 0], b, token_half(s, d)), z_recv.at[d, s, b])
+
+    forward(0, 0, 0)
+    forward(0, 0, 1)
     await_bytes(master_v, l_sem.at[0])
     w16[...] = master_v[...].astype(jnp.bfloat16)
-    await_bytes(ctx_v, l_sem.at[1])
-    ct_own[...] = ctx_v[...].T
-    pl.semaphore_wait(barrier, 23)
-
-    def og(s, t):
-        return og_all.at[s, t]
-
-    def source(s):
-        return og_ref if s == 0 else og_all.at[s, 0]
-
-    def part(ref, b):
-        return ref.at[pl.ds(b * ht, ht)]
-
-    def forward(s, b, d):
-        if d == 0:
-            to, peer = (s - 1) % NZ, z_peer(1)
-        else:
-            to, peer = (s + 1) % NZ, z_peer(NZ - 1)
-        remote(
-            part(source(s), b), part(og_all.at[to, 0], b), z_send, z_recv.at[2 * to + b], peer
-        )
-
-    def to_sibling(s, b):
-        remote(
-            part(source(s), b), part(og_all.at[s, 1], b), s_send, s_recv.at[s], sibling
-        )
-
-    def arrived(s, b):
-        await_bytes(part(og_all.at[s, 0], b), z_recv.at[2 * s + b])
 
     late = lax.div(mod(z + NZ - row, NZ), jnp.int32(4))
 
@@ -177,8 +187,8 @@
             w16.at[w_place(row_to)], w_in.at[row], w_send.at[0], w_recv.at[0], (row_to, z, dep)
         )
     w_in[row] = w16[w_place(row)]
-    forward(0, 0, 0)
-    forward(0, 1, 1)
+    await_bytes(ctx_v, l_sem.at[1])
+    ct_own[...] = ctx_v[...].T
     ct_half = (1 - c) * half
     remote(
         ct_own.at[pl.ds(pl.multiple_of(ct_half, half), half)],
@@ -206,19 +216,23 @@
 
     ct_mine = pl.ds(pl.multiple_of(c * half, half), half)
 
-    def grad_terms(s):
-        total = jnp.dot(ct_own[ct_mine, :], og(s, 0)[...], preferred_element_type=jnp.float32)
-        total += jnp.dot(ct_sib[...], og_all[s, 1], preferred_element_type=jnp.float32)
-        return total.astype(jnp.bfloat16).reshape(4, 4 * U, total.shape[-1])
-
-    def grad_partial(s):
-        await_bytes(og_all.at[s, 1], s_recv.at[s])
-        p_buf[s] = grad_terms(s)
+    def grad_terms(s, b):
+        await_bytes(part(og_all.at[s, 1], b), s_recv.at[s, b])
+        total = jnp.dot(
+            ct_own[ct_mine, :], og_all[s, 0, :, cols[b]], preferred_element_type=jnp.float32
+        )
+        total += jnp.dot(
+            ct_sib[...], og_all[s, 1, :, cols[b]], preferred_element_type=jnp.float32
+        )
+        p_buf[s, :, :, cols[b]] = total.astype(jnp.bfloat16).reshape(4, 4 * U, total.shape[-1])
+
+    def grad_partial(s, b):
+        grad_terms(s, b)
         axis, peer = (x, x_peer) if s < 4 else (y, y_peer)
         for j in range(1, 4):
             remote(
-                p_buf.at[s, mod(axis + j, 4)],
-                r1.at[s, j - 1],
+                p_buf.at[s, mod(axis + j, 4), :, cols[b]],
+                r1.at[s, j - 1, :, cols[b]],
                 r1_send.at[s],
                 r1_recv.at[s],
                 peer(j),
@@ -253,16 +267,15 @@
             f_buf[s] = total.astype(jnp.bfloat16)
             remote(f_buf.at[s], gz.at[s], h_send, h_recv.at[s], z_peer(s))
 
-    def grad_last():
-        await_bytes(og_all.at[4, 1], s_recv.at[4])
-        p_buf[4] = grad_terms(4)
+    def grad_last(b):
+        grad_terms(4, b)
         for jx in range(4):
             for jy in range(4):
                 if jx or jy:
                     xx, yy = mod(x + jx, 4), mod(y + jy, 4)
                     remote(
-                        p_buf.at[4, yy, pl.ds(pl.multiple_of(xx * U, U), U)],
-                        rd.at[jx * 4 + jy - 1],
+                        p_buf.at[4, yy, pl.ds(pl.multiple_of(xx * U, U), U), cols[b]],
+                        rd.at[jx * 4 + jy - 1, :, cols[b]],
                         r1_send.at[4],
                         r1_recv.at[4],
                         (xx * 2 + lax.div(yy, jnp.int32(2)), z, mod(yy, 2) * 2 + c),
@@ -312,82 +325,92 @@
     def w_gathered(parity, n, recv):
         await_bytes(w_pan.at[parity, :, pl.ds(0, 3 * n)], recv)
 
-    def pass_on(s, b, d, onward=True):
-        arrived(s, b)
-        if onward:
+    def pass_on(s, b, d):
+        arrived(s, b, d)
+        if s != 4:
             forward(s, b, d)
-        to_sibling(s, b)
+        to_sibling(s, b, d)
 
     rows_x = pl.ds(pl.multiple_of(x * 4 * U, 4 * U), 4 * U)
     rows_y = pl.ds(pl.multiple_of(y * 4 * U, 4 * U), 4 * U)
 
+    forward(0, 1, 0)
+    forward(0, 1, 1)
+    await_bytes(og_all.at[0, 0], l_sem.at[2])
+    await_bytes(ct_sib, m_recv.at[0])
+    grad_partial(0, 0)
+    grad_partial(0, 1)
+    pass_on(7, 0, 0)
+    pass_on(1, 0, 1)
     await_bytes(w_in.at[pl.ds(0, 7)], w_recv.at[1])
-    forward(0, 1, 0)
-    forward(0, 0, 1)
     w_gather(0, y_peer, pl.ds(place[0], U), U, w_send.at[2], w_recv.at[2])
     w_gather(1, x_peer, pl.ds(place[1], U), U, w_send.at[3], w_recv.at[3])
-    await_bytes(og_all.at[0, 0], l_sem.at[2])
-    await_bytes(ct_sib, m_recv.at[0])
-    pass_on(7, 0, 0)
+    grad_partial(7, 0)
+    grad_partial(1, 0)
+    pass_on(7, 1, 0)
     pass_on(1, 1, 1)
-    grad_partial(0)
     w_gathered(0, U, w_recv.at[2])
     w_gather(0, x_peer, rows_x, 4 * U, w_send.at[4], w_recv.at[4])
     w_gathered(1, U, w_recv.at[3])
     w_gather(1, y_peer, rows_y, 4 * U, w_send.at[5], w_recv.at[5])
-    pass_on(7, 1, 0)
-    pass_on(1, 0, 1)
-    grad_partial(7)
-    grad_partial(1)
+    grad_partial(7, 1)
+    grad_partial(1, 1)
     reduce_first(0)
     pass_on(6, 0, 0)
+    pass_on(2, 0, 1)
+    grad_partial(6, 0)
+    grad_partial(2, 0)
+    pass_on(6, 1, 0)
     pass_on(2, 1, 1)
-    pass_on(6, 1, 0)
-    pass_on(2, 0, 1)
     reduce_first(7)
     reduce_first(1)
-    grad_partial(6)
-    grad_partial(2)
+    grad_partial(6, 1)
+    grad_partial(2, 1)
+    pass_on(5, 0, 0)
+    pass_on(3, 0, 1)
     reduce_second(0)
     reduce_second(7)
     reduce_second(1)
-    pass_on(5, 0, 0)
-    pass_on(3, 1, 1)
-    pass_on(5, 1, 0, onward=False)
-    pass_on(3, 0, 1, onward=False)
+    grad_partial(5, 0)
+    grad_partial(3, 0)
     reduce_first(6)
     reduce_first(2)
-    grad_partial(5)
-    grad_partial(3)
     deliver(0)
+    pass_on(5, 1, 0)
+    pass_on(3, 1, 1)
+    grad_partial(5, 1)
+    grad_partial(3, 1)
+    reduce_second(6)
+    reduce_second(2)
+    w_gathered(0, 4 * U, w_recv.at[4])
+    input_partial(0)
+    pass_on(4, 0, 0)
+    pass_on(4, 0, 1)
+    input_partial(1)
     deliver(7)
     deliver(1)
-    w_gathered(0, 4 * U, w_recv.at[4])
-    input_partial(0)
-    input_partial(1)
+    input_partial(2)
+    grad_last(0)
+    pass_on(4, 1, 0)
+    pass_on(4, 1, 1)
+    reduce_first(5)
+    reduce_first(3)
+    grad_last(1)
     w_gathered(1, 4 * U, w_recv.at[5])
     input_partial(7)
-    reduce_second(6)
-    reduce_second(2)
-    pass_on(4, 0, 0, onward=False)
-    pass_on(4, 1, 1, onward=False)
-    reduce_first(5)
-    reduce_first(3)
-    grad_last()
-    deliver(6)
-    deliver(2)
+    input_partial(6)
     reduce_second(5)
     reduce_second(3)
-    input_partial(2)
-    input_partial(6)
     input_partial(5)
     input_partial(3)
     reduce_last()
-    deliver(5)
-    deliver(3)
+    deliver(6)
+    deliver(2)
     input_partial(4)
     ig_out[...] = acc[1].astype(jnp.bfloat16)
     remote(ig_out, ig_in, m_send.at[1], m_recv.at[1], sibling)
+    deliver(5)
+    deliver(3)
     deliver(4)
     ig_ref[:, ct_mine] = acc[0].astype(jnp.bfloat16)
     ct_other = pl.ds(pl.multiple_of(ct_half, half), half)
@@ -431,8 +454,8 @@
     input_grad, gradient = pl.pallas_call(
         kernel,
         out_shape=(
-            jax.ShapeDtypeStruct((tok, 2 * half), bf16),
-            jax.ShapeDtypeStruct((2 * half, width), bf16),
+            pltpu.VMEM((tok, 2 * half), bf16),
+            pltpu.VMEM((2 * half, width), bf16),
         ),
         in_specs=[pl.BlockSpec(memory_space=pltpu.HBM)] * 3,
         out_specs=(vmem, vmem),
@@ -458,9 +481,9 @@
             pltpu.VMEM((tok, half), bf16),
             pltpu.VMEM((tok, half), bf16),
             dma,
-            dma((2 * NZ,)),
+            dma((2, NZ, 2)),
             dma,
-            dma((NZ,)),
+            dma((NZ, 2)),
             dma((3,)),
             dma((3,)),
             dma((6,)),
@@ -477,7 +500,7 @@
             dma((3,)),
         ],
         compiler_params=pltpu.CompilerParams(
-            collective_id=0, has_side_effects=True, vmem_limit_bytes=60 * 1024 * 1024
+            collective_id=0, has_side_effects=True, vmem_limit_bytes=56 * 1024 * 1024
         ),
         cost_estimate=pl.CostEstimate(
             flops=8 * tok * width * 2 * half * 2, bytes_accessed=4_000_000, transcendentals=0

time: 97 us -> 88.4 us (0.911)
  Pallas kernels: 91.7 us -> 84.2 us
  other arithmetic: 3.7 us -> 2.57 us
    pallas_call x1, Pallas kernels: 91.7 us -> 84.2 us  [on_device(): pl.pallas_call(kernel, out_shape=(pltpu.VMEM((tok, 2 * half), bf16), pltp...]
    sub x1, other arithmetic: 3.7 us -> 2.57 us  [adam_update(): master - learn_rate * (first_hat / (jnp.sqrt(second_hat) + adam_eps) + de...]
where the time goes in v3:
time: 88.4 us; the launch traced here: 88.3 us
  Pallas kernels  84.2 us (95%)
  other arithmetic  2.57 us (3%)
    pallas_call x1, Pallas kernels, on_device(): pl.pallas_call(kernel, out_shape=(pltpu.VMEM((tok, 2 * half), bf16), pltp...  84.2 us
    sub x1, other arithmetic, adam_update(): master - learn_rate * (first_hat / (jnp.sqrt(second_hat) + adam_eps) + de...  2.57 us

profile of v3, /device:TPU:5, one launch (start us, length us, event | category | flops | bytes accessed | tf_op | source)
XLA Modules:
  0.0 88.3 jit_solution(7051757813813845645)
XLA Ops:
  0.6 0.0 copy-start
  0.6 0.0 copy-start.1
  0.7 0.0 copy-start.2
  0.7 84.2 %shard_map.84 = (bf16[512,512]{1,0:T(8,128)(2,1)S(1)}, bf16[512,640]{1,0:T(8,128)(2,1)S(1)}) custom-call(bf16[512,512]{1,0:T(8,128)(2,1)} %ctx_ref.1, bf16[512,640]{1,0:T(8,128)(2,1)} %og_ref.1, f32[512,640]{1,0:T(8,128)} %master_ref.1), custom_call_target="tpu_custom_call" | custom-call | flops 2684354560 | bytes 4000000 | tf_op jit(solution)/shard_map/pallas_call | solution.py:454
  84.9 0.8 copy.10
  85.7 0.0 copy-done
  85.7 0.0 copy-done.1
  85.7 0.0 copy-done.2
  85.7 2.6 %multiply_subtract_fusion = (f32[512,640]{1,0:T(8,128)}, f32[512,640]{1,0:T(8,128)}, f32[512,640]{1,0:T(8,128)}) fusion(f32[512,640]{1,0:T(8,128)S(1)} %copy-done, bf16[512,640]{1,0:T(8,128)(2,1)S(1)} %get-tuple-element.7, f32[512,640]{1,0:T(8,128)S(1)} %copy-done.1, f32[512,640]{1,0:T(8,128)S(1)} %copy-done.2), kind=kLoop, calls=%fused_computation.4 | loop fusion | flops 5242880 | bytes 8519680 | tf_op jit(solution)/shard_map/sub | solution.py:27
Async XLA Ops:
  0.6 85.1 %copy-start = (f32[512,640]{1,0:T(8,128)S(1)}, f32[512,640]{1,0:T(8,128)}, u32[]{:S(2)}) copy-start(f32[512,640]{1,0:T(8,128)} %master_ref.1) | copy-start | bytes 3932164
  0.6 85.1 %copy-start.1 = (f32[512,640]{1,0:T(8,128)S(1)}, f32[512,640]{1,0:T(8,128)}, u32[]{:S(2)}) copy-start(f32[512,640]{1,0:T(8,128)} %param.8) | copy-start | bytes 3932164
  0.7 85.0 %copy-start.2 = (f32[512,640]{1,0:T(8,128)S(1)}, f32[512,640]{1,0:T(8,128)}, u32[]{:S(2)}) copy-start(f32[512,640]{1,0:T(8,128)} %param.9) | copy-start | bytes 3932164

commit v4 on v3

--- a/solution.py
+++ b/solution.py
@@ -15,6 +15,7 @@
 
 MESH = pl.DeviceIdType.MESH
 NZ = 8
+PIECES = 4
 CUT = 256
 U = 16
 
@@ -387,8 +388,6 @@
     pass_on(4, 0, 0)
     pass_on(4, 0, 1)
     input_partial(1)
-    deliver(7)
-    deliver(1)
     input_partial(2)
     grad_last(0)
     pass_on(4, 1, 0)
@@ -404,6 +403,8 @@
     input_partial(5)
     input_partial(3)
     reduce_last()
+    deliver(7)
+    deliver(1)
     deliver(6)
     deliver(2)
     input_partial(4)
@@ -443,6 +444,44 @@
     await_bytes(f_buf.at[pl.ds(0, 7)], h_send)
     await_bytes(gz, f_send)
     await_bytes(gz.at[pl.ds(0, 7)], f_own_send)
+
+
+def update_kernel(
+    input_ref,
+    grad_ref,
+    master_ref,
+    first_ref,
+    second_ref,
+    input_out,
+    master_out,
+    first_out,
+    second_out,
+    master_v,
+    first_v,
+    second_v,
+    input_sem,
+    out_sem,
+):
+    copies = [pltpu.make_async_copy(input_ref, input_out, input_sem)]
+    copies[0].start()
+    n = grad_ref.shape[0] // PIECES
+    for i in range(PIECES):
+        rows = pl.ds(i * n, n)
+        results = adam_update(
+            grad_ref[rows, :].astype(jnp.float32),
+            master_ref[rows, :],
+            first_ref[rows, :],
+            second_ref[rows, :],
+        )
+        held = (master_v, first_v, second_v)
+        outs = (master_out, first_out, second_out)
+        for k in range(3):
+            held[k][rows, :] = results[k]
+            copy = pltpu.make_async_copy(held[k].at[rows], outs[k].at[rows], out_sem.at[i, k])
+            copy.start()
+            copies.append(copy)
+    for copy in copies:
+        copy.wait()
 
 
 def on_device(context, out_grad, master, first_moment, second_moment):
@@ -506,10 +545,25 @@
             flops=8 * tok * width * 2 * half * 2, bytes_accessed=4_000_000, transcendentals=0
         ),
     )(context, out_grad, master)
-    new_master, new_first, new_second = adam_update(
-        gradient.astype(jnp.float32), master, first_moment, second_moment
-    )
-    return (input_grad, new_master, new_first, new_second)
+    hbm = pl.BlockSpec(memory_space=pltpu.HBM)
+    tile = jax.ShapeDtypeStruct(master.shape, jnp.float32)
+    return pl.pallas_call(
+        update_kernel,
+        out_shape=(jax.ShapeDtypeStruct(input_grad.shape, bf16), tile, tile, tile),
+        in_specs=[vmem] * 5,
+        out_specs=(hbm,) * 4,
+        scratch_shapes=[
+            pltpu.VMEM(master.shape, jnp.float32),
+            pltpu.VMEM(master.shape, jnp.float32),
+            pltpu.VMEM(master.shape, jnp.float32),
+            dma,
+            dma((PIECES, 3)),
+        ],
+        compiler_params=pltpu.CompilerParams(vmem_limit_bytes=8 * 1024 * 1024),
+        cost_estimate=pl.CostEstimate(
+            flops=20 * master.size, bytes_accessed=12 * master.size, transcendentals=2 * master.size
+        ),
+    )(input_grad, gradient, master, first_moment, second_moment)
 
 
 def solution(mesh):

time: 88.4 us -> 87.1 us (0.985)
  other arithmetic: 2.57 us -> 0 us
  Pallas kernels: 84.2 us -> 86.3 us
    sub x1 -> x0, other arithmetic: 2.57 us -> none  [adam_update(): master - learn_rate * (first_hat / (jnp.sqrt(second_hat) + adam_eps) + de...]
    pallas_call x0 -> x1, Pallas kernels: none -> 2.29 us  [on_device(): pl.pallas_call(update_kernel, out_shape=(jax.ShapeDtypeStruct(input_grad....]
where the time goes in v4:
time: 87.1 us; the launch traced here: 87 us
  Pallas kernels  86.3 us (99%)
    pallas_call x1, Pallas kernels, on_device(): pl.pallas_call(kernel, out_shape=(pltpu.VMEM((tok, 2 * half), bf16), pltp...  84 us
    pallas_call x1, Pallas kernels, on_device(): pl.pallas_call(update_kernel, out_shape=(jax.ShapeDtypeStruct(input_grad....  2.29 us

profile of v4, /device:TPU:5, one launch (start us, length us, event | category | flops | bytes accessed | tf_op | source)
XLA Modules:
  0.0 87.0 jit_solution(6900814852124641207)
XLA Ops:
  0.6 0.0 copy-start
  0.6 0.0 copy-start.2
  0.7 0.0 copy-start.1
  0.7 84.0 %shard_map.84 = (bf16[512,512]{1,0:T(8,128)(2,1)S(1)}, bf16[512,640]{1,0:T(8,128)(2,1)S(1)}) custom-call(bf16[512,512]{1,0:T(8,128)(2,1)} %ctx_ref.1, bf16[512,640]{1,0:T(8,128)(2,1)} %og_ref.1, f32[512,640]{1,0:T(8,128)} %master_ref.3), custom_call_target="tpu_custom_call" | custom-call | flops 2684354560 | bytes 4000000 | tf_op jit(solution)/shard_map/pallas_call | solution.py:493
  84.7 0.0 copy-done
  84.7 0.0 copy-done.2
  84.7 0.0 copy-done.1
  84.7 2.3 %shard_map.85 = (bf16[512,512]{1,0:T(8,128)(2,1)}, f32[512,640]{1,0:T(8,128)}, f32[512,640]{1,0:T(8,128)}, f32[512,640]{1,0:T(8,128)}) custom-call(bf16[512,512]{1,0:T(8,128)(2,1)S(1)} %get-tuple-element.6.input_ref, bf16[512,640]{1,0:T(8,128)(2,1)S(1)} %get-tuple-element.7.grad_ref, f32[512,640]{1,0:T(8,128)S(1)} %copy-done, f32[512,640]{1,0:T(8,128)S(1)} %copy-done.1, ...), custom_call_target="tpu_custom_call" | custom-call | flops 6553600 | bytes 3932160 | tf_op jit(solution)/shard_map/pallas_call | solution.py:550
Async XLA Ops:
  0.6 84.1 %copy-start = (f32[512,640]{1,0:T(8,128)S(1)}, f32[512,640]{1,0:T(8,128)}, u32[]{:S(2)}) copy-start(f32[512,640]{1,0:T(8,128)} %master_ref.3) | copy-start | bytes 3932164
  0.6 84.1 %copy-start.2 = (f32[512,640]{1,0:T(8,128)S(1)}, f32[512,640]{1,0:T(8,128)}, u32[]{:S(2)}) copy-start(f32[512,640]{1,0:T(8,128)} %second_ref.1) | copy-start | bytes 3932164
  0.7 84.1 %copy-start.1 = (f32[512,640]{1,0:T(8,128)S(1)}, f32[512,640]{1,0:T(8,128)}, u32[]{:S(2)}) copy-start(f32[512,640]{1,0:T(8,128)} %first_ref.1) | copy-start | bytes 3932164

commit v5 on v4

--- a/solution.py
+++ b/solution.py
@@ -79,6 +79,8 @@
     f_own_send,
     f_recv,
     l_sem,
+    d_recv,
+    h_last_recv,
 ):
     row, z, dep = lax.axis_index("row"), lax.axis_index("col"), lax.axis_index("depth")
     x, yh = lax.div(row, jnp.int32(2)), mod(row, 2)
@@ -118,6 +120,9 @@
         pl.multiple_of(y * (4 * U) + x * U, U),
     )
 
+    pltpu.make_async_copy(master_ref, master_v, l_sem.at[0]).start()
+    pltpu.make_async_copy(ctx_ref, ctx_v, l_sem.at[1]).start()
+    pltpu.make_async_copy(og_ref, og_all.at[0, 0], l_sem.at[2]).start()
     barrier = pltpu.get_barrier_semaphore()
     for s in range(1, NZ):
         pl.semaphore_signal(barrier, inc=1, device_id=z_peer(s), device_id_type=MESH)
@@ -131,9 +136,6 @@
                     device_id=(mod(row + j, 8), z, mod(yl + e, 2) * 2 + c),
                     device_id_type=MESH,
                 )
-    pltpu.make_async_copy(master_ref, master_v, l_sem.at[0]).start()
-    pltpu.make_async_copy(ctx_ref, ctx_v, l_sem.at[1]).start()
-    pltpu.make_async_copy(og_ref, og_all.at[0, 0], l_sem.at[2]).start()
     pl.semaphore_wait(barrier, 23)
 
     def og(s, t):
@@ -278,34 +280,38 @@
                         p_buf.at[4, yy, pl.ds(pl.multiple_of(xx * U, U), U), cols[b]],
                         rd.at[jx * 4 + jy - 1, :, cols[b]],
                         r1_send.at[4],
-                        r1_recv.at[4],
+                        d_recv.at[b],
                         (xx * 2 + lax.div(yy, jnp.int32(2)), z, mod(yy, 2) * 2 + c),
                     )
 
-    def reduce_last():
-        await_bytes(rd, r1_recv.at[4])
-        total = p_buf[4, y, pl.ds(pl.multiple_of(x * U, U), U)].astype(jnp.float32)
+    def reduce_last(b):
+        await_bytes(rd.at[:, :, cols[b]], d_recv.at[b])
+        total = p_buf[4, y, pl.ds(pl.multiple_of(x * U, U), U), cols[b]].astype(jnp.float32)
         for j in range(15):
-            total += rd[j].astype(jnp.float32)
-        f_buf[4] = total.astype(jnp.bfloat16)
-        remote(f_buf.at[4], gz.at[4], h_send, h_recv.at[4], z_peer(4))
-
-    def deliver(s):
-        if s:
+            total += rd[j, :, cols[b]].astype(jnp.float32)
+        f_buf[4, :, cols[b]] = total.astype(jnp.bfloat16)
+        remote(
+            f_buf.at[4, :, cols[b]], gz.at[4, :, cols[b]], h_send, h_last_recv.at[b], z_peer(4)
+        )
+
+    def deliver(s, b=None):
+        span = slice(None) if b is None else cols[b]
+        if s == 4:
+            await_bytes(gz.at[4, :, span], h_last_recv.at[b])
+        elif s:
             await_bytes(gz.at[s], h_recv.at[s])
         row_to = mod(z + (NZ - s), NZ)
         spot = pl.ds(place[s // 4], U)
-        remote(
-            gz.at[s], g_tile.at[spot], f_send, f_recv, (row_to, z, (1 - yl) * 2 + c)
-        )
+        source_piece, target = gz.at[s, :, span], g_tile.at[spot, span]
+        remote(source_piece, target, f_send, f_recv, (row_to, z, (1 - yl) * 2 + c))
 
         @pl.when(row_to != row)
         def _():
-            remote(gz.at[s], g_tile.at[spot], f_own_send, f_recv, (row_to, z, dep))
+            remote(source_piece, target, f_own_send, f_recv, (row_to, z, dep))
 
         @pl.when(row_to == row)
         def _():
-            g_tile[spot, :] = gz[s]
+            g_tile[spot, span] = gz[s, :, span]
 
     def input_partial(s):
         w = w_pan[s // 4, s % 4]
@@ -400,9 +406,10 @@
     input_partial(6)
     reduce_second(5)
     reduce_second(3)
+    reduce_last(0)
     input_partial(5)
     input_partial(3)
-    reduce_last()
+    reduce_last(1)
     deliver(7)
     deliver(1)
     deliver(6)
@@ -412,7 +419,8 @@
     remote(ig_out, ig_in, m_send.at[1], m_recv.at[1], sibling)
     deliver(5)
     deliver(3)
-    deliver(4)
+    deliver(4, 0)
+    deliver(4, 1)
     ig_ref[:, ct_mine] = acc[0].astype(jnp.bfloat16)
     ct_other = pl.ds(pl.multiple_of(ct_half, half), half)
 
@@ -537,6 +545,8 @@
             dma,
             dma,
             dma((3,)),
+            dma((2,)),
+            dma((2,)),
         ],
         compiler_params=pltpu.CompilerParams(
             collective_id=0, has_side_effects=True, vmem_limit_bytes=56 * 1024 * 1024

time: 87.1 us -> 86.2 us (0.990)
  Pallas kernels: 86.3 us -> 85.4 us
    pallas_call x1, Pallas kernels: 84 us -> 83.1 us  [on_device(): pl.pallas_call(kernel, out_shape=(pltpu.VMEM((tok, 2 * half), bf16), pltp...]
where the time goes in v5:
time: 86.2 us; the launch traced here: 86.1 us
  Pallas kernels  85.4 us (99%)
    pallas_call x1, Pallas kernels, on_device(): pl.pallas_call(kernel, out_shape=(pltpu.VMEM((tok, 2 * half), bf16), pltp...  83.1 us
    pallas_call x1, Pallas kernels, on_device(): pl.pallas_call(update_kernel, out_shape=(jax.ShapeDtypeStruct(input_grad....  2.29 us

profile of v5, /device:TPU:5, one launch (start us, length us, event | category | flops | bytes accessed | tf_op | source)
XLA Modules:
  0.0 86.1 jit_solution(8660130969117335266)
XLA Ops:
  0.6 0.0 copy-start
  0.6 0.0 copy-start.2
  0.7 0.0 copy-start.1
  0.7 83.1 %shard_map.84 = (bf16[512,512]{1,0:T(8,128)(2,1)S(1)}, bf16[512,640]{1,0:T(8,128)(2,1)S(1)}) custom-call(bf16[512,512]{1,0:T(8,128)(2,1)} %ctx_ref.1, bf16[512,640]{1,0:T(8,128)(2,1)} %og_ref.1, f32[512,640]{1,0:T(8,128)} %master_ref.3), custom_call_target="tpu_custom_call" | custom-call | flops 2684354560 | bytes 4000000 | tf_op jit(solution)/shard_map/pallas_call | solution.py:501
  83.8 0.0 copy-done
  83.8 0.0 copy-done.2
  83.8 0.0 copy-done.1
  83.8 2.3 %shard_map.85 = (bf16[512,512]{1,0:T(8,128)(2,1)}, f32[512,640]{1,0:T(8,128)}, f32[512,640]{1,0:T(8,128)}, f32[512,640]{1,0:T(8,128)}) custom-call(bf16[512,512]{1,0:T(8,128)(2,1)S(1)} %get-tuple-element.6.input_ref, bf16[512,640]{1,0:T(8,128)(2,1)S(1)} %get-tuple-element.7.grad_ref, f32[512,640]{1,0:T(8,128)S(1)} %copy-done, f32[512,640]{1,0:T(8,128)S(1)} %copy-done.1, ...), custom_call_target="tpu_custom_call" | custom-call | flops 6553600 | bytes 3932160 | tf_op jit(solution)/shard_map/pallas_call | solution.py:560
Async XLA Ops:
  0.6 83.1 %copy-start = (f32[512,640]{1,0:T(8,128)S(1)}, f32[512,640]{1,0:T(8,128)}, u32[]{:S(2)}) copy-start(f32[512,640]{1,0:T(8,128)} %master_ref.3) | copy-start | bytes 3932164
  0.6 83.1 %copy-start.2 = (f32[512,640]{1,0:T(8,128)S(1)}, f32[512,640]{1,0:T(8,128)}, u32[]{:S(2)}) copy-start(f32[512,640]{1,0:T(8,128)} %second_ref.1) | copy-start | bytes 3932164
  0.7 83.1 %copy-start.1 = (f32[512,640]{1,0:T(8,128)S(1)}, f32[512,640]{1,0:T(8,128)}, u32[]{:S(2)}) copy-start(f32[512,640]{1,0:T(8,128)} %first_ref.1) | copy-start | bytes 3932164

commit v6 on v5

--- a/solution.py
+++ b/solution.py
@@ -272,8 +272,8 @@
 
     def grad_last(b):
         grad_terms(4, b)
-        for jx in range(4):
-            for jy in range(4):
+        for jx in (2, 1, 3, 0):
+            for jy in (2, 1, 3, 0):
                 if jx or jy:
                     xx, yy = mod(x + jx, 4), mod(y + jy, 4)
                     remote(
@@ -369,10 +369,10 @@
     grad_partial(2, 0)
     pass_on(6, 1, 0)
     pass_on(2, 1, 1)
+    grad_partial(6, 1)
+    grad_partial(2, 1)
     reduce_first(7)
     reduce_first(1)
-    grad_partial(6, 1)
-    grad_partial(2, 1)
     pass_on(5, 0, 0)
     pass_on(3, 0, 1)
     reduce_second(0)

time: 86.2 us -> 85.9 us (level)
  no operation moved by 1% of the time
where the time goes in v6:
time: 85.9 us; the launch traced here: 85.8 us
  Pallas kernels  85.1 us (99%)
    pallas_call x1, Pallas kernels, on_device(): pl.pallas_call(kernel, out_shape=(pltpu.VMEM((tok, 2 * half), bf16), pltp...  82.8 us
    pallas_call x1, Pallas kernels, on_device(): pl.pallas_call(update_kernel, out_shape=(jax.ShapeDtypeStruct(input_grad....  2.29 us

profile of v6, /device:TPU:5, one launch (start us, length us, event | category | flops | bytes accessed | tf_op | source)
XLA Modules:
  0.0 85.8 jit_solution(16986370635804029221)
XLA Ops:
  0.6 0.0 copy-start
  0.6 0.0 copy-start.2
  0.7 0.0 copy-start.1
  0.7 82.8 %shard_map.84 = (bf16[512,512]{1,0:T(8,128)(2,1)S(1)}, bf16[512,640]{1,0:T(8,128)(2,1)S(1)}) custom-call(bf16[512,512]{1,0:T(8,128)(2,1)} %ctx_ref.1, bf16[512,640]{1,0:T(8,128)(2,1)} %og_ref.1, f32[512,640]{1,0:T(8,128)} %master_ref.3), custom_call_target="tpu_custom_call" | custom-call | flops 2684354560 | bytes 4000000 | tf_op jit(solution)/shard_map/pallas_call | solution.py:501
  83.5 0.0 copy-done
  83.5 0.0 copy-done.2
  83.5 0.0 copy-done.1
  83.5 2.3 %shard_map.85 = (bf16[512,512]{1,0:T(8,128)(2,1)}, f32[512,640]{1,0:T(8,128)}, f32[512,640]{1,0:T(8,128)}, f32[512,640]{1,0:T(8,128)}) custom-call(bf16[512,512]{1,0:T(8,128)(2,1)S(1)} %get-tuple-element.6.input_ref, bf16[512,640]{1,0:T(8,128)(2,1)S(1)} %get-tuple-element.7.grad_ref, f32[512,640]{1,0:T(8,128)S(1)} %copy-done, f32[512,640]{1,0:T(8,128)S(1)} %copy-done.1, ...), custom_call_target="tpu_custom_call" | custom-call | flops 6553600 | bytes 3932160 | tf_op jit(solution)/shard_map/pallas_call | solution.py:560
Async XLA Ops:
  0.6 82.9 %copy-start = (f32[512,640]{1,0:T(8,128)S(1)}, f32[512,640]{1,0:T(8,128)}, u32[]{:S(2)}) copy-start(f32[512,640]{1,0:T(8,128)} %master_ref.3) | copy-start | bytes 3932164
  0.6 82.9 %copy-start.2 = (f32[512,640]{1,0:T(8,128)S(1)}, f32[512,640]{1,0:T(8,128)}, u32[]{:S(2)}) copy-start(f32[512,640]{1,0:T(8,128)} %second_ref.1) | copy-start | bytes 3932164
  0.7 82.9 %copy-start.1 = (f32[512,640]{1,0:T(8,128)S(1)}, f32[512,640]{1,0:T(8,128)}, u32[]{:S(2)}) copy-start(f32[512,640]{1,0:T(8,128)} %first_ref.1) | copy-start | bytes 3932164
